TPU v7x, 32 devices: a whole 2x2x4 slice. The times are simulated.
32 devices in a mesh: dom: 16 (over z, y, x), sub: 2 (over core).
Axes of the slice: x: 2, y: 2, z: 4, core: 2. Of those that a mesh axis runs over, the one named last changes fastest.
Arguments:
- jac_blocks: bfloat16 [384, 6, 128, 128], P(('dom', 'sub')), may hold values from -0.06717514 to 0.06717514
- block_cols: int32 [384, 6], P(('dom', 'sub')), may hold values from 0 to 19, as said below
- precond: float32 [384, 36, 128], P(('dom', 'sub')), may hold values from -0.3 to 0.3
- right_side: float32 [384, 48, 128], P(('dom', 'sub')), may hold values from -6 to 6
- halo_rows: int32 [128, 2], P(('dom', 'sub')), may hold values from 0 to 11
- surface_tile: int32 [256], P(('dom', 'sub')), may hold values from 0 to 11
- surface_block: int32 [256], P(('dom', 'sub')), may hold values from 0 to 7
- surface_count: int32 [32], P(('dom', 'sub')), may hold values from 0 to 8, as said below
- surface_residual_derivative: float32 [256, 18, 128], P(('dom', 'sub')), may hold values from -6 to 6
- lattice_bernstein_weights: bfloat16 [256, 128, 128], P(('dom', 'sub')), may hold values from 0 to 0.03125
Outputs:
- adjoint: float32 [384, 48, 128], P(('dom', 'sub'))
- design_grad: float32 [2, 8, 24, 128], P(None, 'sub')
Inputs may be any that keep to these rules, and one draw needn't show every extreme that they name: `block_cols`: entries below 12 name the partition's own tiles; entry 12 + k * 2 + h names halo tile h of neighbour k. `surface_count`: slots at and beyond the count are empty; some partition has all 8 slots live.
All inputs are finite; a program needn't handle non-finite values.
Results may differ from a plain program's by a relative error of at most 0.0055.
Values may be sent and summed in bfloat16 or wider, within the bound.
A program may use at most 64 MiB of HBM per device.

v0:
```python
import math

import jax
import jax.numpy as jnp
from jax import lax
from jax.sharding import PartitionSpec as P

NOBJ = 8
NVAR = 6
FB_DEV = 4
OUTER = 2
INNER = 5


OFFSETS = (1, -1, 2, -2)
RELAXATION = 0.7


def from_behind(value, axis, steps):
    count = lax.axis_size(axis)
    pairs = [(source, (source + steps) % count) for source in range(count)]
    return lax.ppermute(value, axis, pairs)


def variable_mix(blending_factor, residual):
    tile_count = residual.shape[0]
    cell_count = residual.shape[-1]
    residual_split = residual.reshape(tile_count, NOBJ, NVAR, cell_count)
    mixing_split = blending_factor.reshape(tile_count, NVAR, NVAR, cell_count)
    mixed = jnp.sum(mixing_split[:, None, :, :, :] * residual_split[:, :, None, :, :], axis=3)
    return mixed.reshape(tile_count, NOBJ * NVAR, cell_count)


def design_partial(
    adjoint,
    surface_tile,
    surface_block,
    surface_count,
    surface_residual_derivative,
    lattice_bernstein_weights,
):
    slot_count = surface_tile.shape[0]
    cell_count = adjoint.shape[-1]
    block_total = FB_DEV * lax.axis_size("sub")
    selected = adjoint[surface_tile]
    weights_split = surface_residual_derivative.reshape(slot_count, 1, NVAR, 3, cell_count)
    sensitivity = jnp.sum(
        selected.reshape(slot_count, NOBJ, NVAR, 1, cell_count) * weights_split, axis=2
    )
    alive = (jnp.arange(slot_count, dtype=jnp.int32) < surface_count[0]).astype(jnp.float32)
    rounded = (
        (sensitivity * alive[:, None, None, None])
        .reshape(slot_count, NOBJ * 3, cell_count)
        .astype(jnp.bfloat16)
    )
    projected = jnp.einsum(
        "uoc,upc->uop", rounded, lattice_bernstein_weights, preferred_element_type=jnp.float32
    )
    selector = (surface_block[:, None] == jnp.arange(block_total, dtype=jnp.int32)[None, :]).astype(
        jnp.float32
    )
    return jnp.einsum("ub,uop->bop", selector, projected, precision=lax.Precision.HIGHEST)


def per_device(
    jac_blocks,
    block_cols,
    precond,
    right_side,
    halo_rows,
    surface_tile,
    surface_block,
    surface_count,
    surface_residual_derivative,
    lattice_bernstein_weights,
):
    slot_count = surface_tile.shape[0]
    scaling = math.sqrt(FB_DEV / (slot_count * lax.axis_size("dom")))
    adjoint = jnp.zeros_like(right_side)
    gradients = []
    for outer_index in range(OUTER):
        for sweep_index in range(INNER):
            rounded = adjoint.astype(jnp.bfloat16)
            halo_tiles = []
            for position, offset in enumerate(OFFSETS):
                neighbour = from_behind(rounded, "dom", offset)
                halo_tiles.append(neighbour[halo_rows[position]])
            extended = jnp.concatenate([rounded] + halo_tiles, axis=0)
            picked = extended[block_cols]
            coupled = adjoint + jnp.einsum(
                "tbor,tbrc->toc", picked, jac_blocks, preferred_element_type=jnp.float32
            )
            residual = right_side - coupled
            adjoint = adjoint + RELAXATION * residual + variable_mix(precond, residual)
        partial_sum = design_partial(
            adjoint,
            surface_tile,
            surface_block,
            surface_count,
            surface_residual_derivative,
            lattice_bernstein_weights,
        )
        summed = lax.psum(partial_sum, ("dom", "sub"))
        fraction_part = lax.dynamic_slice_in_dim(summed, lax.axis_index("sub") * FB_DEV, FB_DEV, 0)
        gradients.append(fraction_part * scaling)
    return (adjoint, jnp.stack(gradients, axis=0))


def solution(mesh):
    in_specs = (
        P(("dom", "sub"), None, None, None),
        P(("dom", "sub"), None),
        P(("dom", "sub"), None, None),
        P(("dom", "sub"), None, None),
        P(("dom", "sub"), None),
        P(("dom", "sub")),
        P(("dom", "sub")),
        P(("dom", "sub")),
        P(("dom", "sub"), None, None),
        P(("dom", "sub"), None, None),
    )
    out_specs = (P(("dom", "sub"), None, None), P(None, "sub", None, None))
    return jax.shard_map(
        per_device, mesh=mesh, in_specs=in_specs, out_specs=out_specs, check_vma=False
    )
```

profile of v0, /device:TPU:0, one launch (start us, length us, event | category | flops | bytes accessed | tf_op | source)
XLA Modules:
  0.0 430.0 jit_solution(2997908801800547792)
XLA Ops:
  7.3 3.0 collective-permute-start
  10.3 4.1 collective-permute-start.1
  14.3 4.7 %collective-permute-start.3 = (bf16[12,48,128]{2,1,0:T(8,128)(2,1)S(1)}, bf16[12,48,128]{2,1,0:T(8,128)(2,1)S(1)}, u32[]{:S(2)}, u32[]{:S(2)}) collective-permute-start(bf16[12,48,128]{2,1,0:T(8,128)(2,1)S(1)} %broadcast_in_dim.6), channel_id=1, source_target_pairs={{0,28},{2,30},{4,0},{6,2},{8,4},{10,6},{12,8},{14,10},{16,12},{18,... | collective-permute-start | bytes 442376 | tf_op jit(solution)/shard_map/ppermute | solution.py:22
  35.2 5.6 %collective-permute-start.5 = (bf16[12,48,128]{2,1,0:T(8,128)(2,1)}, bf16[12,48,128]{2,1,0:T(8,128)(2,1)}, u32[]{:S(2)}, u32[]{:S(2)}) collective-permute-start(bf16[12,48,128]{2,1,0:T(8,128)(2,1)} %get-tuple-element.41), channel_id=1, source_target_pairs={{0,30},{2,0},{4,2},{6,4},{8,6},{10,8},{12,10},{14,12},{16,14},{18,... | collective-permute-start | bytes 442376 | tf_op jit(solution)/shard_map/ppermute | solution.py:22
  40.8 4.7 %collective-permute-start.7 = (bf16[12,48,128]{2,1,0:T(8,128)(2,1)}, bf16[12,48,128]{2,1,0:T(8,128)(2,1)}, u32[]{:S(2)}, u32[]{:S(2)}) collective-permute-start(bf16[12,48,128]{2,1,0:T(8,128)(2,1)} %get-tuple-element.41), channel_id=1, source_target_pairs={{0,28},{2,30},{4,0},{6,2},{8,4},{10,6},{12,8},{14,10},{16,12},{18,... | collective-permute-start | bytes 442376 | tf_op jit(solution)/shard_map/ppermute | solution.py:22
  46.0 2.2 gather_fusion.5
  49.5 2.1 gather_fusion.6
  53.0 2.1 gather_fusion.7
  56.4 2.1 gather_fusion.8
  59.8 2.6 gather_fusion.9
  62.4 2.4 fusion.17
  72.3 5.6 %collective-permute-start.9 = (bf16[12,48,128]{2,1,0:T(8,128)(2,1)}, bf16[12,48,128]{2,1,0:T(8,128)(2,1)}, u32[]{:S(2)}, u32[]{:S(2)}) collective-permute-start(bf16[12,48,128]{2,1,0:T(8,128)(2,1)} %get-tuple-element.38), channel_id=1, source_target_pairs={{0,30},{2,0},{4,2},{6,4},{8,6},{10,8},{12,10},{14,12},{16,14},{18,... | collective-permute-start | bytes 442376 | tf_op jit(solution)/shard_map/ppermute | solution.py:22
  78.0 4.7 %collective-permute-start.11 = (bf16[12,48,128]{2,1,0:T(8,128)(2,1)}, bf16[12,48,128]{2,1,0:T(8,128)(2,1)S(1)}, u32[]{:S(2)}, u32[]{:S(2)}) collective-permute-start(bf16[12,48,128]{2,1,0:T(8,128)(2,1)} %get-tuple-element.38), channel_id=1, source_target_pairs={{0,28},{2,30},{4,0},{6,2},{8,4},{10,6},{12,8},{14,10},{16,12},{18,... | collective-permute-start | bytes 442376 | tf_op jit(solution)/shard_map/ppermute | solution.py:22
  90.2 2.6 gather_fusion.14
  92.8 2.4 fusion.15
  102.7 5.6 %collective-permute-start.13 = (bf16[12,48,128]{2,1,0:T(8,128)(2,1)}, bf16[12,48,128]{2,1,0:T(8,128)(2,1)}, u32[]{:S(2)}, u32[]{:S(2)}) collective-permute-start(bf16[12,48,128]{2,1,0:T(8,128)(2,1)} %get-tuple-element.35), channel_id=1, source_target_pairs={{0,30},{2,0},{4,2},{6,4},{8,6},{10,8},{12,10},{14,12},{16,14},{18,... | collective-permute-start | bytes 442376 | tf_op jit(solution)/shard_map/ppermute | solution.py:22
  108.3 4.7 %collective-permute-start.15 = (bf16[12,48,128]{2,1,0:T(8,128)(2,1)}, bf16[12,48,128]{2,1,0:T(8,128)(2,1)}, u32[]{:S(2)}, u32[]{:S(2)}) collective-permute-start(bf16[12,48,128]{2,1,0:T(8,128)(2,1)} %get-tuple-element.35), channel_id=1, source_target_pairs={{0,28},{2,30},{4,0},{6,2},{8,4},{10,6},{12,8},{14,10},{16,12},{18,... | collective-permute-start | bytes 442376 | tf_op jit(solution)/shard_map/ppermute | solution.py:22
  121.1 2.4 fusion.13
  130.9 5.6 %collective-permute-start.17 = (bf16[12,48,128]{2,1,0:T(8,128)(2,1)}, bf16[12,48,128]{2,1,0:T(8,128)(2,1)}, u32[]{:S(2)}, u32[]{:S(2)}) collective-permute-start(bf16[12,48,128]{2,1,0:T(8,128)(2,1)} %get-tuple-element.32), channel_id=1, source_target_pairs={{0,30},{2,0},{4,2},{6,4},{8,6},{10,8},{12,10},{14,12},{16,14},{18,... | collective-permute-start | bytes 442376 | tf_op jit(solution)/shard_map/ppermute | solution.py:22
  136.5 4.7 %collective-permute-start.19 = (bf16[12,48,128]{2,1,0:T(8,128)(2,1)}, bf16[12,48,128]{2,1,0:T(8,128)(2,1)}, u32[]{:S(2)}, u32[]{:S(2)}) collective-permute-start(bf16[12,48,128]{2,1,0:T(8,128)(2,1)} %get-tuple-element.32), channel_id=1, source_target_pairs={{0,28},{2,30},{4,0},{6,2},{8,4},{10,6},{12,8},{14,10},{16,12},{18,... | collective-permute-start | bytes 442376 | tf_op jit(solution)/shard_map/ppermute | solution.py:22
  149.3 2.5 fusion.11
  155.7 5.6 %collective-permute-start.21 = (bf16[12,48,128]{2,1,0:T(8,128)(2,1)}, bf16[12,48,128]{2,1,0:T(8,128)(2,1)}, u32[]{:S(2)}, u32[]{:S(2)}) collective-permute-start(bf16[12,48,128]{2,1,0:T(8,128)(2,1)} %get-tuple-element.29), channel_id=1, source_target_pairs={{0,30},{2,0},{4,2},{6,4},{8,6},{10,8},{12,10},{14,12},{16,14},{18,... | collective-permute-start | bytes 442376 | tf_op jit(solution)/shard_map/ppermute | solution.py:22
  161.3 4.7 %collective-permute-start.23 = (bf16[12,48,128]{2,1,0:T(8,128)(2,1)}, bf16[12,48,128]{2,1,0:T(8,128)(2,1)}, u32[]{:S(2)}, u32[]{:S(2)}) collective-permute-start(bf16[12,48,128]{2,1,0:T(8,128)(2,1)} %get-tuple-element.29), channel_id=1, source_target_pairs={{0,28},{2,30},{4,0},{6,2},{8,4},{10,6},{12,8},{14,10},{16,12},{18,... | collective-permute-start | bytes 442376 | tf_op jit(solution)/shard_map/ppermute | solution.py:22
  182.4 5.6 %collective-permute-start.25 = (bf16[12,48,128]{2,1,0:T(8,128)(2,1)}, bf16[12,48,128]{2,1,0:T(8,128)(2,1)}, u32[]{:S(2)}, u32[]{:S(2)}) collective-permute-start(bf16[12,48,128]{2,1,0:T(8,128)(2,1)} %get-tuple-element.26), channel_id=1, source_target_pairs={{0,30},{2,0},{4,2},{6,4},{8,6},{10,8},{12,10},{14,12},{16,14},{18,... | collective-permute-start | bytes 442376 | tf_op jit(solution)/shard_map/ppermute | solution.py:22
  188.0 4.7 %collective-permute-start.27 = (bf16[12,48,128]{2,1,0:T(8,128)(2,1)}, bf16[12,48,128]{2,1,0:T(8,128)(2,1)}, u32[]{:S(2)}, u32[]{:S(2)}) collective-permute-start(bf16[12,48,128]{2,1,0:T(8,128)(2,1)} %get-tuple-element.26), channel_id=1, source_target_pairs={{0,28},{2,30},{4,0},{6,2},{8,4},{10,6},{12,8},{14,10},{16,12},{18,... | collective-permute-start | bytes 442376 | tf_op jit(solution)/shard_map/ppermute | solution.py:22
  209.2 5.6 %collective-permute-start.29 = (bf16[12,48,128]{2,1,0:T(8,128)(2,1)}, bf16[12,48,128]{2,1,0:T(8,128)(2,1)}, u32[]{:S(2)}, u32[]{:S(2)}) collective-permute-start(bf16[12,48,128]{2,1,0:T(8,128)(2,1)} %get-tuple-element.23), channel_id=1, source_target_pairs={{0,30},{2,0},{4,2},{6,4},{8,6},{10,8},{12,10},{14,12},{16,14},{18,... | collective-permute-start | bytes 442376 | tf_op jit(solution)/shard_map/ppermute | solution.py:22
  214.9 4.7 %collective-permute-start.31 = (bf16[12,48,128]{2,1,0:T(8,128)(2,1)}, bf16[12,48,128]{2,1,0:T(8,128)(2,1)}, u32[]{:S(2)}, u32[]{:S(2)}) collective-permute-start(bf16[12,48,128]{2,1,0:T(8,128)(2,1)} %get-tuple-element.23), channel_id=1, source_target_pairs={{0,28},{2,30},{4,0},{6,2},{8,4},{10,6},{12,8},{14,10},{16,12},{18,... | collective-permute-start | bytes 442376 | tf_op jit(solution)/shard_map/ppermute | solution.py:22
  236.1 5.6 %collective-permute-start.33 = (bf16[12,48,128]{2,1,0:T(8,128)(2,1)}, bf16[12,48,128]{2,1,0:T(8,128)(2,1)}, u32[]{:S(2)}, u32[]{:S(2)}) collective-permute-start(bf16[12,48,128]{2,1,0:T(8,128)(2,1)} %get-tuple-element.20), channel_id=1, source_target_pairs={{0,30},{2,0},{4,2},{6,4},{8,6},{10,8},{12,10},{14,12},{16,14},{18,... | collective-permute-start | bytes 442376 | tf_op jit(solution)/shard_map/ppermute | solution.py:22
  242.9 4.7 %collective-permute-start.35 = (bf16[12,48,128]{2,1,0:T(8,128)(2,1)}, bf16[12,48,128]{2,1,0:T(8,128)(2,1)}, u32[]{:S(2)}, u32[]{:S(2)}) collective-permute-start(bf16[12,48,128]{2,1,0:T(8,128)(2,1)} %get-tuple-element.20), channel_id=1, source_target_pairs={{0,28},{2,30},{4,0},{6,2},{8,4},{10,6},{12,8},{14,10},{16,12},{18,... | collective-permute-start | bytes 442376 | tf_op jit(solution)/shard_map/ppermute | solution.py:22
  265.4 5.7 %collective-permute-start.37 = (bf16[12,48,128]{2,1,0:T(8,128)(2,1)}, bf16[12,48,128]{2,1,0:T(8,128)(2,1)}, u32[]{:S(2)}, u32[]{:S(2)}) collective-permute-start(bf16[12,48,128]{2,1,0:T(8,128)(2,1)} %get-tuple-element.17), channel_id=1, source_target_pairs={{0,30},{2,0},{4,2},{6,4},{8,6},{10,8},{12,10},{14,12},{16,14},{18,... | collective-permute-start | bytes 442376 | tf_op jit(solution)/shard_map/ppermute | solution.py:22
  276.2 4.7 %collective-permute-start.39 = (bf16[12,48,128]{2,1,0:T(8,128)(2,1)}, bf16[12,48,128]{2,1,0:T(8,128)(2,1)}, u32[]{:S(2)}, u32[]{:S(2)}) collective-permute-start(bf16[12,48,128]{2,1,0:T(8,128)(2,1)} %get-tuple-element.17), channel_id=1, source_target_pairs={{0,28},{2,30},{4,0},{6,2},{8,4},{10,6},{12,8},{14,10},{16,12},{18,... | collective-permute-start | bytes 442376 | tf_op jit(solution)/shard_map/ppermute | solution.py:22
  298.9 122.6 %all-reduce.3.cloned.1.call-done = (f32[8,24,128]{2,0,1:T(8,128)}, f32[8,24,128]{2,0,1:T(8,128)}) async-done(((f32[8,24,128]{2,0,1:T(8,128)}, f32[8,24,128]{2,0,1:T(8,128)}), (f32[8,24,128]{2,0,1:T(8,128)}, f32[8,24,128]{2,0,1:T(8,128)})) %all-reduce.3.cloned.1.call-update) | async-done | bytes 196624 | tf_op jit(solution)/shard_map/psum | solution.py:103
  (280 shorter events, 163.7 us)
Async XLA Ops:
  7.2 414.3 %all-reduce.3.cloned.1.call-start = ((), (), s32[]{:S(2)}) async-start(), calls=%async_computation | async-start | bytes 393216 | tf_op jit(solution)/shard_map/psum | solution.py:103
  7.3 14.8 %collective-permute-start = (bf16[12,48,128]{2,1,0:T(8,128)(2,1)S(1)}, bf16[12,48,128]{2,1,0:T(8,128)(2,1)}, u32[]{:S(2)}, u32[]{:S(2)}) collective-permute-start(bf16[12,48,128]{2,1,0:T(8,128)(2,1)S(1)} %broadcast_in_dim.6), channel_id=1, source_target_pairs={{0,2},{2,4},{4,6},{6,8},{8,10},{10,12},{12,14},{14,16},{16,18},{18... | collective-permute-start | bytes 442376 | tf_op jit(solution)/shard_map/ppermute | solution.py:22
  10.3 13.3 %collective-permute-start.1 = (bf16[12,48,128]{2,1,0:T(8,128)(2,1)S(1)}, bf16[12,48,128]{2,1,0:T(8,128)(2,1)}, u32[]{:S(2)}, u32[]{:S(2)}) collective-permute-start(bf16[12,48,128]{2,1,0:T(8,128)(2,1)S(1)} %broadcast_in_dim.6), channel_id=1, source_target_pairs={{0,30},{2,0},{4,2},{6,4},{8,6},{10,8},{12,10},{14,12},{16,14},{18,... | collective-permute-start | bytes 442376 | tf_op jit(solution)/shard_map/ppermute | solution.py:22
  14.3 10.7 %collective-permute-start.2 = (bf16[12,48,128]{2,1,0:T(8,128)(2,1)S(1)}, bf16[12,48,128]{2,1,0:T(8,128)(2,1)}, u32[]{:S(2)}, u32[]{:S(2)}) collective-permute-start(bf16[12,48,128]{2,1,0:T(8,128)(2,1)S(1)} %broadcast_in_dim.6), channel_id=1, source_target_pairs={{0,4},{2,6},{4,8},{6,10},{8,12},{10,14},{12,16},{14,18},{16,20},{1... | collective-permute-start | bytes 442376 | tf_op jit(solution)/shard_map/ppermute | solution.py:22
  14.3 12.2 %collective-permute-start.3 = (bf16[12,48,128]{2,1,0:T(8,128)(2,1)S(1)}, bf16[12,48,128]{2,1,0:T(8,128)(2,1)S(1)}, u32[]{:S(2)}, u32[]{:S(2)}) collective-permute-start(bf16[12,48,128]{2,1,0:T(8,128)(2,1)S(1)} %broadcast_in_dim.6), channel_id=1, source_target_pairs={{0,28},{2,30},{4,0},{6,2},{8,4},{10,6},{12,8},{14,10},{16,12},{18,... | collective-permute-start | bytes 442376 | tf_op jit(solution)/shard_map/ppermute | solution.py:22
  35.2 10.9 %collective-permute-start.4 = (bf16[12,48,128]{2,1,0:T(8,128)(2,1)}, bf16[12,48,128]{2,1,0:T(8,128)(2,1)}, u32[]{:S(2)}, u32[]{:S(2)}) collective-permute-start(bf16[12,48,128]{2,1,0:T(8,128)(2,1)} %get-tuple-element.41), channel_id=1, source_target_pairs={{0,2},{2,4},{4,6},{6,8},{8,10},{10,12},{12,14},{14,16},{16,18},{18... | collective-permute-start | bytes 442376 | tf_op jit(solution)/shard_map/ppermute | solution.py:22
  35.2 14.4 %collective-permute-start.5 = (bf16[12,48,128]{2,1,0:T(8,128)(2,1)}, bf16[12,48,128]{2,1,0:T(8,128)(2,1)}, u32[]{:S(2)}, u32[]{:S(2)}) collective-permute-start(bf16[12,48,128]{2,1,0:T(8,128)(2,1)} %get-tuple-element.41), channel_id=1, source_target_pairs={{0,30},{2,0},{4,2},{6,4},{8,6},{10,8},{12,10},{14,12},{16,14},{18,... | collective-permute-start | bytes 442376 | tf_op jit(solution)/shard_map/ppermute | solution.py:22
  40.8 12.2 %collective-permute-start.6 = (bf16[12,48,128]{2,1,0:T(8,128)(2,1)}, bf16[12,48,128]{2,1,0:T(8,128)(2,1)}, u32[]{:S(2)}, u32[]{:S(2)}) collective-permute-start(bf16[12,48,128]{2,1,0:T(8,128)(2,1)} %get-tuple-element.41), channel_id=1, source_target_pairs={{0,4},{2,6},{4,8},{6,10},{8,12},{10,14},{12,16},{14,18},{16,20},{1... | collective-permute-start | bytes 442376 | tf_op jit(solution)/shard_map/ppermute | solution.py:22
  40.8 15.6 %collective-permute-start.7 = (bf16[12,48,128]{2,1,0:T(8,128)(2,1)}, bf16[12,48,128]{2,1,0:T(8,128)(2,1)}, u32[]{:S(2)}, u32[]{:S(2)}) collective-permute-start(bf16[12,48,128]{2,1,0:T(8,128)(2,1)} %get-tuple-element.41), channel_id=1, source_target_pairs={{0,28},{2,30},{4,0},{6,2},{8,4},{10,6},{12,8},{14,10},{16,12},{18,... | collective-permute-start | bytes 442376 | tf_op jit(solution)/shard_map/ppermute | solution.py:22
  72.3 10.3 %collective-permute-start.8 = (bf16[12,48,128]{2,1,0:T(8,128)(2,1)}, bf16[12,48,128]{2,1,0:T(8,128)(2,1)}, u32[]{:S(2)}, u32[]{:S(2)}) collective-permute-start(bf16[12,48,128]{2,1,0:T(8,128)(2,1)} %get-tuple-element.38), channel_id=1, source_target_pairs={{0,2},{2,4},{4,6},{6,8},{8,10},{10,12},{12,14},{14,16},{16,18},{18... | collective-permute-start | bytes 442376 | tf_op jit(solution)/shard_map/ppermute | solution.py:22
  72.3 12.5 %collective-permute-start.9 = (bf16[12,48,128]{2,1,0:T(8,128)(2,1)}, bf16[12,48,128]{2,1,0:T(8,128)(2,1)}, u32[]{:S(2)}, u32[]{:S(2)}) collective-permute-start(bf16[12,48,128]{2,1,0:T(8,128)(2,1)} %get-tuple-element.38), channel_id=1, source_target_pairs={{0,30},{2,0},{4,2},{6,4},{8,6},{10,8},{12,10},{14,12},{16,14},{18,... | collective-permute-start | bytes 442376 | tf_op jit(solution)/shard_map/ppermute | solution.py:22
  78.0 11.1 %collective-permute-start.11 = (bf16[12,48,128]{2,1,0:T(8,128)(2,1)}, bf16[12,48,128]{2,1,0:T(8,128)(2,1)S(1)}, u32[]{:S(2)}, u32[]{:S(2)}) collective-permute-start(bf16[12,48,128]{2,1,0:T(8,128)(2,1)} %get-tuple-element.38), channel_id=1, source_target_pairs={{0,28},{2,30},{4,0},{6,2},{8,4},{10,6},{12,8},{14,10},{16,12},{18,... | collective-permute-start | bytes 442376 | tf_op jit(solution)/shard_map/ppermute | solution.py:22
  102.7 10.3 %collective-permute-start.12 = (bf16[12,48,128]{2,1,0:T(8,128)(2,1)}, bf16[12,48,128]{2,1,0:T(8,128)(2,1)}, u32[]{:S(2)}, u32[]{:S(2)}) collective-permute-start(bf16[12,48,128]{2,1,0:T(8,128)(2,1)} %get-tuple-element.35), channel_id=1, source_target_pairs={{0,2},{2,4},{4,6},{6,8},{8,10},{10,12},{12,14},{14,16},{16,18},{18... | collective-permute-start | bytes 442376 | tf_op jit(solution)/shard_map/ppermute | solution.py:22
  102.7 12.0 %collective-permute-start.13 = (bf16[12,48,128]{2,1,0:T(8,128)(2,1)}, bf16[12,48,128]{2,1,0:T(8,128)(2,1)}, u32[]{:S(2)}, u32[]{:S(2)}) collective-permute-start(bf16[12,48,128]{2,1,0:T(8,128)(2,1)} %get-tuple-element.35), channel_id=1, source_target_pairs={{0,30},{2,0},{4,2},{6,4},{8,6},{10,8},{12,10},{14,12},{16,14},{18,... | collective-permute-start | bytes 442376 | tf_op jit(solution)/shard_map/ppermute | solution.py:22
  108.3 9.6 %collective-permute-start.15 = (bf16[12,48,128]{2,1,0:T(8,128)(2,1)}, bf16[12,48,128]{2,1,0:T(8,128)(2,1)}, u32[]{:S(2)}, u32[]{:S(2)}) collective-permute-start(bf16[12,48,128]{2,1,0:T(8,128)(2,1)} %get-tuple-element.35), channel_id=1, source_target_pairs={{0,28},{2,30},{4,0},{6,2},{8,4},{10,6},{12,8},{14,10},{16,12},{18,... | collective-permute-start | bytes 442376 | tf_op jit(solution)/shard_map/ppermute | solution.py:22
  130.9 10.3 %collective-permute-start.16 = (bf16[12,48,128]{2,1,0:T(8,128)(2,1)}, bf16[12,48,128]{2,1,0:T(8,128)(2,1)}, u32[]{:S(2)}, u32[]{:S(2)}) collective-permute-start(bf16[12,48,128]{2,1,0:T(8,128)(2,1)} %get-tuple-element.32), channel_id=1, source_target_pairs={{0,2},{2,4},{4,6},{6,8},{8,10},{10,12},{12,14},{14,16},{16,18},{18... | collective-permute-start | bytes 442376 | tf_op jit(solution)/shard_map/ppermute | solution.py:22
  130.9 12.0 %collective-permute-start.17 = (bf16[12,48,128]{2,1,0:T(8,128)(2,1)}, bf16[12,48,128]{2,1,0:T(8,128)(2,1)}, u32[]{:S(2)}, u32[]{:S(2)}) collective-permute-start(bf16[12,48,128]{2,1,0:T(8,128)(2,1)} %get-tuple-element.32), channel_id=1, source_target_pairs={{0,30},{2,0},{4,2},{6,4},{8,6},{10,8},{12,10},{14,12},{16,14},{18,... | collective-permute-start | bytes 442376 | tf_op jit(solution)/shard_map/ppermute | solution.py:22
  136.5 9.6 %collective-permute-start.19 = (bf16[12,48,128]{2,1,0:T(8,128)(2,1)}, bf16[12,48,128]{2,1,0:T(8,128)(2,1)}, u32[]{:S(2)}, u32[]{:S(2)}) collective-permute-start(bf16[12,48,128]{2,1,0:T(8,128)(2,1)} %get-tuple-element.32), channel_id=1, source_target_pairs={{0,28},{2,30},{4,0},{6,2},{8,4},{10,6},{12,8},{14,10},{16,12},{18,... | collective-permute-start | bytes 442376 | tf_op jit(solution)/shard_map/ppermute | solution.py:22
  155.7 10.3 %collective-permute-start.20 = (bf16[12,48,128]{2,1,0:T(8,128)(2,1)}, bf16[12,48,128]{2,1,0:T(8,128)(2,1)}, u32[]{:S(2)}, u32[]{:S(2)}) collective-permute-start(bf16[12,48,128]{2,1,0:T(8,128)(2,1)} %get-tuple-element.29), channel_id=1, source_target_pairs={{0,2},{2,4},{4,6},{6,8},{8,10},{10,12},{12,14},{14,16},{16,18},{18... | collective-permute-start | bytes 442376 | tf_op jit(solution)/shard_map/ppermute | solution.py:22
  155.7 12.0 %collective-permute-start.21 = (bf16[12,48,128]{2,1,0:T(8,128)(2,1)}, bf16[12,48,128]{2,1,0:T(8,128)(2,1)}, u32[]{:S(2)}, u32[]{:S(2)}) collective-permute-start(bf16[12,48,128]{2,1,0:T(8,128)(2,1)} %get-tuple-element.29), channel_id=1, source_target_pairs={{0,30},{2,0},{4,2},{6,4},{8,6},{10,8},{12,10},{14,12},{16,14},{18,... | collective-permute-start | bytes 442376 | tf_op jit(solution)/shard_map/ppermute | solution.py:22
  161.3 9.6 %collective-permute-start.23 = (bf16[12,48,128]{2,1,0:T(8,128)(2,1)}, bf16[12,48,128]{2,1,0:T(8,128)(2,1)}, u32[]{:S(2)}, u32[]{:S(2)}) collective-permute-start(bf16[12,48,128]{2,1,0:T(8,128)(2,1)} %get-tuple-element.29), channel_id=1, source_target_pairs={{0,28},{2,30},{4,0},{6,2},{8,4},{10,6},{12,8},{14,10},{16,12},{18,... | collective-permute-start | bytes 442376 | tf_op jit(solution)/shard_map/ppermute | solution.py:22
  182.4 10.3 %collective-permute-start.24 = (bf16[12,48,128]{2,1,0:T(8,128)(2,1)}, bf16[12,48,128]{2,1,0:T(8,128)(2,1)}, u32[]{:S(2)}, u32[]{:S(2)}) collective-permute-start(bf16[12,48,128]{2,1,0:T(8,128)(2,1)} %get-tuple-element.26), channel_id=1, source_target_pairs={{0,2},{2,4},{4,6},{6,8},{8,10},{10,12},{12,14},{14,16},{16,18},{18... | collective-permute-start | bytes 442376 | tf_op jit(solution)/shard_map/ppermute | solution.py:22
  182.4 12.0 %collective-permute-start.25 = (bf16[12,48,128]{2,1,0:T(8,128)(2,1)}, bf16[12,48,128]{2,1,0:T(8,128)(2,1)}, u32[]{:S(2)}, u32[]{:S(2)}) collective-permute-start(bf16[12,48,128]{2,1,0:T(8,128)(2,1)} %get-tuple-element.26), channel_id=1, source_target_pairs={{0,30},{2,0},{4,2},{6,4},{8,6},{10,8},{12,10},{14,12},{16,14},{18,... | collective-permute-start | bytes 442376 | tf_op jit(solution)/shard_map/ppermute | solution.py:22
  188.0 9.6 %collective-permute-start.27 = (bf16[12,48,128]{2,1,0:T(8,128)(2,1)}, bf16[12,48,128]{2,1,0:T(8,128)(2,1)}, u32[]{:S(2)}, u32[]{:S(2)}) collective-permute-start(bf16[12,48,128]{2,1,0:T(8,128)(2,1)} %get-tuple-element.26), channel_id=1, source_target_pairs={{0,28},{2,30},{4,0},{6,2},{8,4},{10,6},{12,8},{14,10},{16,12},{18,... | collective-permute-start | bytes 442376 | tf_op jit(solution)/shard_map/ppermute | solution.py:22
  209.2 10.3 %collective-permute-start.28 = (bf16[12,48,128]{2,1,0:T(8,128)(2,1)}, bf16[12,48,128]{2,1,0:T(8,128)(2,1)}, u32[]{:S(2)}, u32[]{:S(2)}) collective-permute-start(bf16[12,48,128]{2,1,0:T(8,128)(2,1)} %get-tuple-element.23), channel_id=1, source_target_pairs={{0,2},{2,4},{4,6},{6,8},{8,10},{10,12},{12,14},{14,16},{16,18},{18... | collective-permute-start | bytes 442376 | tf_op jit(solution)/shard_map/ppermute | solution.py:22
  209.2 12.0 %collective-permute-start.29 = (bf16[12,48,128]{2,1,0:T(8,128)(2,1)}, bf16[12,48,128]{2,1,0:T(8,128)(2,1)}, u32[]{:S(2)}, u32[]{:S(2)}) collective-permute-start(bf16[12,48,128]{2,1,0:T(8,128)(2,1)} %get-tuple-element.23), channel_id=1, source_target_pairs={{0,30},{2,0},{4,2},{6,4},{8,6},{10,8},{12,10},{14,12},{16,14},{18,... | collective-permute-start | bytes 442376 | tf_op jit(solution)/shard_map/ppermute | solution.py:22
  214.9 9.6 %collective-permute-start.31 = (bf16[12,48,128]{2,1,0:T(8,128)(2,1)}, bf16[12,48,128]{2,1,0:T(8,128)(2,1)}, u32[]{:S(2)}, u32[]{:S(2)}) collective-permute-start(bf16[12,48,128]{2,1,0:T(8,128)(2,1)} %get-tuple-element.23), channel_id=1, source_target_pairs={{0,28},{2,30},{4,0},{6,2},{8,4},{10,6},{12,8},{14,10},{16,12},{18,... | collective-permute-start | bytes 442376 | tf_op jit(solution)/shard_map/ppermute | solution.py:22
  236.1 11.5 %collective-permute-start.32 = (bf16[12,48,128]{2,1,0:T(8,128)(2,1)}, bf16[12,48,128]{2,1,0:T(8,128)(2,1)}, u32[]{:S(2)}, u32[]{:S(2)}) collective-permute-start(bf16[12,48,128]{2,1,0:T(8,128)(2,1)} %get-tuple-element.20), channel_id=1, source_target_pairs={{0,2},{2,4},{4,6},{6,8},{8,10},{10,12},{12,14},{14,16},{16,18},{18... | collective-permute-start | bytes 442376 | tf_op jit(solution)/shard_map/ppermute | solution.py:22
  236.1 13.1 %collective-permute-start.33 = (bf16[12,48,128]{2,1,0:T(8,128)(2,1)}, bf16[12,48,128]{2,1,0:T(8,128)(2,1)}, u32[]{:S(2)}, u32[]{:S(2)}) collective-permute-start(bf16[12,48,128]{2,1,0:T(8,128)(2,1)} %get-tuple-element.20), channel_id=1, source_target_pairs={{0,30},{2,0},{4,2},{6,4},{8,6},{10,8},{12,10},{14,12},{16,14},{18,... | collective-permute-start | bytes 442376 | tf_op jit(solution)/shard_map/ppermute | solution.py:22
  242.9 9.6 %collective-permute-start.35 = (bf16[12,48,128]{2,1,0:T(8,128)(2,1)}, bf16[12,48,128]{2,1,0:T(8,128)(2,1)}, u32[]{:S(2)}, u32[]{:S(2)}) collective-permute-start(bf16[12,48,128]{2,1,0:T(8,128)(2,1)} %get-tuple-element.20), channel_id=1, source_target_pairs={{0,28},{2,30},{4,0},{6,2},{8,4},{10,6},{12,8},{14,10},{16,12},{18,... | collective-permute-start | bytes 442376 | tf_op jit(solution)/shard_map/ppermute | solution.py:22
  264.1 16.9 %collective-permute-start.36 = (bf16[12,48,128]{2,1,0:T(8,128)(2,1)}, bf16[12,48,128]{2,1,0:T(8,128)(2,1)}, u32[]{:S(2)}, u32[]{:S(2)}) collective-permute-start(bf16[12,48,128]{2,1,0:T(8,128)(2,1)} %get-tuple-element.17), channel_id=1, source_target_pairs={{0,2},{2,4},{4,6},{6,8},{8,10},{10,12},{12,14},{14,16},{16,18},{18... | collective-permute-start | bytes 442376 | tf_op jit(solution)/shard_map/ppermute | solution.py:22
  265.4 17.1 %collective-permute-start.37 = (bf16[12,48,128]{2,1,0:T(8,128)(2,1)}, bf16[12,48,128]{2,1,0:T(8,128)(2,1)}, u32[]{:S(2)}, u32[]{:S(2)}) collective-permute-start(bf16[12,48,128]{2,1,0:T(8,128)(2,1)} %get-tuple-element.17), channel_id=1, source_target_pairs={{0,30},{2,0},{4,2},{6,4},{8,6},{10,8},{12,10},{14,12},{16,14},{18,... | collective-permute-start | bytes 442376 | tf_op jit(solution)/shard_map/ppermute | solution.py:22
  (25 other events, 368.5 us)
Sparse Core Ops, SparseCore 0:
  299.0 122.4 all-reduce.2
where the time goes:
time: 433 us; the launch traced here: 430 us
  local copies, waits for them, and re-layouts  138 us (32%)
  waiting for transfers between devices  125 us (29%)
  starting transfers between devices  105 us (24%)
  other arithmetic  24 us (6%)
  matrix products  22.5 us (5%)
  between operations  15.4 us (4%)
    psum x1, waiting for transfers between devices, per_device(): summed = lax.psum(partial_sum, ('dom', 'sub'))  123 us
    ppermute x40, starting transfers between devices, from_behind(): return lax.ppermute(value, axis, pairs)  105 us
    gather x40, local copies, waits for them, and re-layouts, per_device(): halo_tiles.append(neighbour[halo_rows[position]])  60.4 us
    mul x21, local copies, waits for them, and re-layouts, variable_mix(): mixing_split[:, None, :, :, :] * residual_split[:, :, None, :, :]  21.8 us
    dot_general x10, matrix products, per_device(): jnp.einsum('tbor,tbrc->toc', picked, jac_blocks, preferred_element_type=j...  20.3 us
    gather x10, local copies, waits for them, and re-layouts, per_device(): picked = extended[block_cols]  18.4 us
    unnamed x9, other arithmetic  16 us
    reshape x10, local copies, waits for them, and re-layouts, variable_mix(): return mixed.reshape(tile_count, NOBJ * NVAR, cell_count)  14.7 us
  transfers between devices with their start and end apart: 41, of which 9 were waited for; matrix products, arithmetic and copies ran while one was open for 15% of the time, Pallas kernels for 0%

commit v1 on v0

v1 whole, which is shorter than its diff:
```python
import functools
import math

import jax
import jax.numpy as jnp
from jax import lax
from jax.experimental import pallas as pl
from jax.experimental.pallas import tpu as pltpu
from jax.sharding import PartitionSpec as P

NOBJ = 8
NVAR = 6
NDIR = 3
OUTER = 2
INNER = 5

OFFSETS = (1, -1, 2, -2)
RELAXATION = 0.7
MESH = pl.DeviceIdType.MESH


def mixed(pre_ref, tile, residual):
    out = []
    for v in range(NVAR):
        total = RELAXATION * residual[v]
        for w in range(NVAR):
            total = total + pre_ref[tile, pl.ds(v * NVAR + w, 1), :] * residual[w]
        out.append(total)
    return out


def kernel(
    n_dom, n_sub, scaling,
    jac_hbm, pre_hbm, rhs_hbm, srd_hbm, weights_hbm,
    cols_ref, halo_ref, surf_tile_ref, surf_block_ref, count_ref,
    adj_out, grad_out,
    jac_ref, pre_ref, rhs_in, srd_ref, weights_ref,
    rhs_ref, adj_ref, ext_ref, send_buf, recv_buf,
    want_out, want_in, want_ref,
    part_ref, sub_buf, acc_ref, dom_buf,
    load_sem, want_send, want_recv, want_local, halo_send, halo_recv,
    sub_send, sub_recv, dom_send, dom_recv,
):
    tiles = adj_ref.shape[0]
    blocks = cols_ref.shape[0] // tiles
    cells = adj_ref.shape[-1]
    halo = recv_buf.shape[2]
    slots = srd_ref.shape[0]
    fb_dev = grad_out.shape[1]
    rows = NOBJ * NVAR
    a = lax.axis_index("dom")
    s = lax.axis_index("sub")

    def shifted(offset):
        return lax.rem(a + offset + n_dom, n_dom)

    loads = [
        pltpu.make_async_copy(src, dst, load_sem.at[number])
        for number, (src, dst) in enumerate((
            (rhs_hbm, rhs_in), (pre_hbm, pre_ref), (jac_hbm, jac_ref),
            (srd_hbm, srd_ref), (weights_hbm, weights_ref)))
    ]
    for load in loads:
        load.start()

    dom_steps = n_dom.bit_length() - 1
    partners = [a + 2 ** k * (1 - 2 * lax.rem(a // 2 ** k, 2)) for k in range(dom_steps)]
    greet = [(shifted(offset), s) for offset in OFFSETS]
    greet += [(partners[k], s) for k in range(2, dom_steps)]
    greet += [(a, lax.rem(s + d, n_sub)) for d in range(1, n_sub)]
    barrier = pltpu.get_barrier_semaphore()
    for device in greet:
        pl.semaphore_signal(barrier, inc=1, device_id=device, device_id_type=MESH)

    lane = lax.broadcasted_iota(jnp.int32, want_out.shape[1:], 1)
    for k in range(len(OFFSETS)):
        demand = jnp.zeros(want_out.shape[1:], jnp.int32)
        for h in range(halo):
            demand = jnp.where(lane == h, halo_ref[k * halo + h], demand)
        want_out[k] = demand
    pl.semaphore_wait(barrier, len(greet))

    def want_copy(k):
        return pltpu.make_async_remote_copy(
            src_ref=want_out.at[k], dst_ref=want_in.at[k],
            send_sem=want_send.at[k], recv_sem=want_recv.at[k],
            device_id=(shifted(-OFFSETS[k]), s), device_id_type=MESH)

    for k in range(len(OFFSETS)):
        want_copy(k).start()

    loads[0].wait()
    loads[1].wait()

    def first(i, carry):
        residual = []
        for v in range(NVAR):
            value = rhs_in[i, pl.ds(v, NOBJ, stride=NVAR), :]
            rhs_ref[i, v] = value
            residual.append(value)
        for v, change in enumerate(mixed(pre_ref, i, residual)):
            adj_ref[i, v] = change
        return carry

    lax.fori_loop(0, tiles, first, 0)

    for k in range(len(OFFSETS)):
        want_copy(k).wait()
    to_smem = pltpu.make_async_copy(want_in, want_ref, want_local)
    to_smem.start()
    to_smem.wait()
    loads[2].wait()

    def sweep(number, between=None):
        parity = lax.rem(number, 2)

        def halo_copy(k):
            return pltpu.make_async_remote_copy(
                src_ref=send_buf.at[k], dst_ref=recv_buf.at[parity, k],
                send_sem=halo_send.at[k], recv_sem=halo_recv.at[parity, k],
                device_id=(shifted(OFFSETS[k]), s), device_id_type=MESH)

        for k in (3, 2, 1, 0):
            for h in range(halo):
                tile = adj_ref[want_ref[k, 0, h]]
                send_buf[k, h] = tile.reshape(rows, cells).astype(jnp.bfloat16)
            halo_copy(k).start()
        for i in range(tiles):
            ext_ref[i] = adj_ref[i].reshape(rows, cells).astype(jnp.bfloat16)
        if between is not None:
            between()
        for k in range(len(OFFSETS)):
            halo_copy(k).wait()
            for h in range(halo):
                ext_ref[tiles + k * halo + h] = recv_buf[parity, k, h]

        group = math.gcd(tiles, 4)

        def some(g, carry):
            for sub_tile in range(group):
                i = g * group + sub_tile
                picked = jnp.concatenate(
                    [ext_ref[cols_ref[i * blocks + b]] for b in range(blocks)], axis=1)
                product = jnp.dot(picked, jac_ref[i], preferred_element_type=jnp.float32)
                current = [adj_ref[i, v] for v in range(NVAR)]
                residual = [
                    rhs_ref[i, v] - (current[v] + product[v * NOBJ:(v + 1) * NOBJ])
                    for v in range(NVAR)
                ]
                for v, change in enumerate(mixed(pre_ref, i, residual)):
                    adj_ref[i, v] = current[v] + change
            return carry

        lax.fori_loop(0, tiles // group, some, 0)

    def design(iteration):
        projected = []
        for u in range(slots):
            alive = jnp.where(u < count_ref[0], 1.0, 0.0).astype(jnp.float32)
            selected = adj_ref[surf_tile_ref[u]]
            parts = []
            for k in range(NDIR):
                total = selected[0] * srd_ref[u, pl.ds(k, 1), :]
                for v in range(1, NVAR):
                    total = total + selected[v] * srd_ref[u, pl.ds(v * NDIR + k, 1), :]
                parts.append(total * alive)
            rounded = jnp.concatenate(parts, axis=0).astype(jnp.bfloat16)
            projected.append(lax.dot_general(
                rounded, weights_ref[u], (((1,), (1,)), ((), ())),
                preferred_element_type=jnp.float32))
        for owner in range(n_sub):
            for f in range(fb_dev):
                total = jnp.zeros_like(projected[0])
                for u in range(slots):
                    chosen = jnp.where(surf_block_ref[u] == owner * fb_dev + f, 1.0, 0.0)
                    total = total + chosen.astype(jnp.float32) * projected[u]
                part_ref[owner, iteration, f] = total

    def looped(number, carry):
        sweep(number)
        return carry

    lax.fori_loop(0, INNER - 1, looped, 0)
    loads[3].wait()
    loads[4].wait()
    sweep(INNER - 1, lambda: design(0))
    lax.fori_loop(INNER, 2 * INNER - 1, looped, 0)
    design(1)

    def sub_copy(d):
        other = lax.rem(s + d, n_sub)
        return pltpu.make_async_remote_copy(
            src_ref=part_ref.at[other], dst_ref=sub_buf.at[d - 1],
            send_sem=sub_send.at[d - 1], recv_sem=sub_recv.at[d - 1],
            device_id=(a, other), device_id_type=MESH)

    def dom_copy(k):
        return pltpu.make_async_remote_copy(
            src_ref=acc_ref.at[k], dst_ref=dom_buf.at[k],
            send_sem=dom_send.at[k], recv_sem=dom_recv.at[k],
            device_id=(partners[k], s), device_id_type=MESH)

    for d in range(1, n_sub):
        sub_copy(d).start()
    for i in range(tiles):
        for v in range(NVAR):
            adj_out[i, pl.ds(v, NOBJ, stride=NVAR), :] = adj_ref[i, v]
    total = part_ref[s]
    for d in range(1, n_sub):
        sub_copy(d).wait()
        total = total + sub_buf[d - 1]
    for k in range(dom_steps):
        acc_ref[k] = total
        dom_copy(k).start()
        dom_copy(k).wait()
        total = acc_ref[k] + dom_buf[k]
    total = total * scaling
    for iteration in range(OUTER):
        for f in range(fb_dev):
            for k in range(NDIR):
                grad_out[iteration, f, pl.ds(k, NOBJ, stride=NDIR), :] = (
                    total[iteration, f, k * NOBJ:(k + 1) * NOBJ])


def per_device(
    n_dom,
    n_sub,
    block_total,
    jac_blocks,
    block_cols,
    precond,
    right_side,
    halo_rows,
    surface_tile,
    surface_block,
    surface_count,
    surface_residual_derivative,
    lattice_bernstein_weights,
):
    tiles, blocks, cells, _ = jac_blocks.shape
    slots, controls, _ = lattice_bernstein_weights.shape
    neighbours, halo = halo_rows.shape
    fb_dev = block_total // n_sub
    rows = NOBJ * NVAR
    scaling = math.sqrt(fb_dev / (slots * n_dom))
    dom_steps = n_dom.bit_length() - 1
    grad_rows = NOBJ * NDIR
    f32, bf16, i32 = jnp.float32, jnp.bfloat16, jnp.int32
    dma = pltpu.SemaphoreType.DMA
    anywhere = pl.BlockSpec(memory_space=pl.ANY)
    scalars = pl.BlockSpec(memory_space=pltpu.SMEM)
    vmem = pl.BlockSpec(memory_space=pltpu.VMEM)
    return pl.pallas_call(
        functools.partial(kernel, n_dom, n_sub, scaling),
        out_shape=(
            jax.ShapeDtypeStruct((tiles, rows, cells), f32),
            jax.ShapeDtypeStruct((OUTER, fb_dev, grad_rows, controls), f32),
        ),
        in_specs=[anywhere] * 5 + [scalars] * 5,
        out_specs=(vmem, vmem),
        scratch_shapes=[
            pltpu.VMEM((tiles, blocks * cells, cells), bf16),
            pltpu.VMEM(precond.shape, f32),
            pltpu.VMEM(right_side.shape, f32),
            pltpu.VMEM(surface_residual_derivative.shape, f32),
            pltpu.VMEM(lattice_bernstein_weights.shape, bf16),
            pltpu.VMEM((tiles, NVAR, NOBJ, cells), f32),
            pltpu.VMEM((tiles, NVAR, NOBJ, cells), f32),
            pltpu.VMEM((tiles + neighbours * halo, rows, cells), bf16),
            pltpu.VMEM((neighbours, halo, rows, cells), bf16),
            pltpu.VMEM((2, neighbours, halo, rows, cells), bf16),
            pltpu.VMEM((neighbours, 8, 128), i32),
            pltpu.VMEM((neighbours, 8, 128), i32),
            pltpu.SMEM((neighbours, 8, 128), i32),
            pltpu.VMEM((n_sub, OUTER, fb_dev, grad_rows, controls), f32),
            pltpu.VMEM((n_sub - 1, OUTER, fb_dev, grad_rows, controls), f32),
            pltpu.VMEM((dom_steps, OUTER, fb_dev, grad_rows, controls), f32),
            pltpu.VMEM((dom_steps, OUTER, fb_dev, grad_rows, controls), f32),
            dma((5,)),
            dma((neighbours,)),
            dma((neighbours,)),
            dma,
            dma((neighbours,)),
            dma((2, neighbours)),
            dma((n_sub - 1,)),
            dma((n_sub - 1,)),
            dma((dom_steps,)),
            dma((dom_steps,)),
        ],
        compiler_params=pltpu.CompilerParams(
            collective_id=0, has_side_effects=True, vmem_limit_bytes=40 * 1024 * 1024),
    )(
        jac_blocks.reshape(tiles, blocks * cells, cells),
        precond,
        right_side,
        surface_residual_derivative,
        lattice_bernstein_weights,
        block_cols.reshape(-1),
        halo_rows.reshape(-1),
        surface_tile,
        surface_block,
        surface_count,
    )


FB_DEV = 4


def solution(mesh):
    n_dom, n_sub = mesh.shape["dom"], mesh.shape["sub"]
    both = ("dom", "sub")
    in_specs = (
        P(both, None, None, None),
        P(both, None),
        P(both, None, None),
        P(both, None, None),
        P(both, None),
        P(both),
        P(both),
        P(both),
        P(both, None, None),
        P(both, None, None),
    )
    out_specs = (P(both, None, None), P(None, "sub", None, None))
    return jax.shard_map(
        functools.partial(per_device, n_dom, n_sub, FB_DEV * n_sub),
        mesh=mesh, in_specs=in_specs, out_specs=out_specs, check_vma=False,
    )
```

time: 433 us -> 92.6 us (0.21)
  local copies, waits for them, and re-layouts: 138 us -> 9.79 us
  waiting for transfers between devices: 125 us -> 0 us
  starting transfers between devices: 105 us -> 0 us
  Pallas kernels: 0 us -> 81.1 us
  other arithmetic: 24 us -> 0 us
  matrix products: 22.5 us -> 0 us
  between operations: 15.4 us -> 1.3 us
    psum x1 -> x0, waiting for transfers between devices: 123 us -> none  [per_device(): summed = lax.psum(partial_sum, ('dom', 'sub'))]
    ppermute x40 -> x0, starting transfers between devices: 105 us -> none  [from_behind(): return lax.ppermute(value, axis, pairs)]
    gather x54 -> x0, local copies, waits for them, and re-layouts: 81.9 us -> none  [the longest x40 60.4 us: per_device(): halo_tiles.append(neighbour[halo_rows[position]])]
    pallas_call x0 -> x1, Pallas kernels: none -> 81.1 us  [per_device(): pl.pallas_call(functools.partial(kernel, n_dom, n_sub, scaling), out_shap...]
    mul x24 -> x0, local copies, waits for them, and re-layouts: 24.1 us -> none  [the longest x21 21.8 us: variable_mix(): mixing_split[:, None, :, :, :] * residual_split[:, :, None, :, :]]
    dot_general x14 -> x0, matrix products: 22.5 us -> none  [the longest x10 20.3 us: per_device(): jnp.einsum('tbor,tbrc->toc', picked, jac_blocks, preferred_element_type=j...]
    unnamed x9 -> x0, other arithmetic: 16 us -> none
    reshape x10 -> x2, local copies, waits for them, and re-layouts: 14.7 us -> 0.17 us  [the longest x1 0.08 us: per_device(): halo_rows.reshape(-1)]
  transfers between devices with their start and end apart: 41 -> 0, of which waited for: 9 -> 0; matrix products, arithmetic and copies ran while one was open for 15% -> 0% of each run, Pallas kernels for 0% -> 0%
where the time goes in v1:
time: 92.6 us; the launch traced here: 92.2 us
  Pallas kernels  81.1 us (88%)
  local copies, waits for them, and re-layouts  9.79 us (11%)
  between operations  1.3 us (1%)
    pallas_call x1, Pallas kernels, per_device(): pl.pallas_call(functools.partial(kernel, n_dom, n_sub, scaling), out_shap...  81.1 us
    unnamed x17, local copies, waits for them, and re-layouts  9.63 us

profile of v1, /device:TPU:0, one launch (start us, length us, event | category | flops | bytes accessed | tf_op | source)
XLA Modules:
  0.0 92.2 jit_solution(2898948461688885322)
XLA Ops:
  1.3 0.8 copy.16
  2.0 0.1 reshape.15.halo_ref
  2.1 0.8 copy.15
  2.9 0.1 reshape.14.cols_ref
  3.0 0.9 copy.17.srd_hbm
  3.9 0.0 copy-start
  3.9 1.7 %copy-done = bf16[12,6,128,128]{3,2,1,0:T(8,128)(2,1)S(1)} copy-done((bf16[12,6,128,128]{3,2,1,0:T(8,128)(2,1)S(1)}, bf16[12,6,128,128]{3,2,1,0:T(8,128)(2,1)}, u32[]{:S(2)}) %copy-start) | copy-done | bytes 2359320
  5.6 0.0 copy-start.1
  5.6 1.0 %copy-done.1 = f32[12,48,128]{2,1,0:T(8,128)S(1)} copy-done((f32[12,48,128]{2,1,0:T(8,128)S(1)}, f32[12,48,128]{2,1,0:T(8,128)}, u32[]{:S(2)}) %copy-start.1) | copy-done | bytes 294936
  6.5 0.0 copy-start.2
  6.5 0.9 %copy-done.2 = bf16[8,128,128]{2,1,0:T(8,128)(2,1)S(1)} copy-done((bf16[8,128,128]{2,1,0:T(8,128)(2,1)S(1)}, bf16[8,128,128]{2,1,0:T(8,128)(2,1)}, u32[]{:S(2)}) %copy-start.2) | copy-done | bytes 262168
  7.5 0.0 copy-start.3
  7.5 0.9 %copy-done.3 = f32[12,36,128]{2,1,0:T(8,128)S(1)} copy-done((f32[12,36,128]{2,1,0:T(8,128)S(1)}, f32[12,36,128]{2,1,0:T(8,128)}, u32[]{:S(2)}) %copy-start.3) | copy-done | bytes 221208
  8.4 0.0 copy-start.4
  8.4 0.7 copy-done.4
  9.1 0.0 copy-start.5
  9.1 0.7 copy-done.5
  9.7 81.1 %shard_map.113 = (f32[12,48,128]{2,1,0:T(8,128)S(1)}, f32[2,4,24,128]{3,2,1,0:T(8,128)S(1)}) custom-call(bf16[12,768,128]{2,1,0:T(8,128)(2,1)S(1)} %bitcast.1, f32[12,36,128]{2,1,0:T(8,128)S(1)} %copy-done.3, f32[12,48,128]{2,1,0:T(8,128)S(1)} %copy-done.1, f32[8,18,128]{2,1,0:T(8,128)S(1)} %copy.17.srd_hbm, bf16[8,128,128]{2,1,0:T(8,128)(2,1)S(1)} %copy-done.2, ...), custom_call_target="tpu_custom_call" | custom-call | tf_op jit(solution)/shard_map/pallas_call | solution.py:253
  90.9 0.7 copy.21
  91.6 0.6 copy.22
Async XLA Ops:
  3.9 1.7 %copy-start = (bf16[12,6,128,128]{3,2,1,0:T(8,128)(2,1)S(1)}, bf16[12,6,128,128]{3,2,1,0:T(8,128)(2,1)}, u32[]{:S(2)}) copy-start(bf16[12,6,128,128]{3,2,1,0:T(8,128)(2,1)} %param.10) | copy-start | bytes 7077892
  5.6 1.0 %copy-start.1 = (f32[12,48,128]{2,1,0:T(8,128)S(1)}, f32[12,48,128]{2,1,0:T(8,128)}, u32[]{:S(2)}) copy-start(f32[12,48,128]{2,1,0:T(8,128)} %rhs_hbm.1) | copy-start | bytes 884740
  6.5 0.9 %copy-start.2 = (bf16[8,128,128]{2,1,0:T(8,128)(2,1)S(1)}, bf16[8,128,128]{2,1,0:T(8,128)(2,1)}, u32[]{:S(2)}) copy-start(bf16[8,128,128]{2,1,0:T(8,128)(2,1)} %weights_hbm.1) | copy-start | bytes 786436
  7.5 0.9 %copy-start.3 = (f32[12,36,128]{2,1,0:T(8,128)S(1)}, f32[12,36,128]{2,1,0:T(8,128)}, u32[]{:S(2)}) copy-start(f32[12,36,128]{2,1,0:T(8,128)} %pre_hbm.1) | copy-start | bytes 663556
  8.4 0.7 copy-start.4
  9.1 0.7 copy-start.5

commit v2 on v1

v2 whole, which is shorter than its diff:
```python
import functools
import math

import jax
import jax.numpy as jnp
from jax import lax
from jax.experimental import pallas as pl
from jax.experimental.pallas import tpu as pltpu
from jax.sharding import PartitionSpec as P

NOBJ = 8
NVAR = 6
NDIR = 3
OUTER = 2
INNER = 5

OFFSETS = (1, -1, 2, -2)
RELAXATION = 0.7
MESH = pl.DeviceIdType.MESH


def mixed(pre_ref, tile, residual):
    out = []
    for v in range(NVAR):
        total = RELAXATION * residual[v]
        for w in range(NVAR):
            total = total + pre_ref[tile, pl.ds(v * NVAR + w, 1), :] * residual[w]
        out.append(total)
    return out


def kernel(
    n_dom, n_sub, scaling,
    jac_hbm, pre_hbm, rhs_hbm, srd_hbm, weights_hbm,
    cols_hbm, halo_hbm, surf_tile_hbm, surf_block_hbm, count_hbm,
    adj_out, grad_out,
    jac_ref, pre_ref, rhs_in, srd_ref, weights_ref,
    cols_ref, halo_ref, surf_tile_ref, surf_block_ref, count_ref,
    rhs_ref, adj_ref, ext_ref, send_buf, recv_buf,
    want_out, want_in, want_ref,
    part_ref, sub_buf, acc_ref, dom_buf,
    load_sem, want_send, want_recv, want_local, halo_send, halo_recv,
    sub_send, sub_recv, dom_send, dom_recv,
):
    blocks, tiles = cols_ref.shape
    cells = adj_ref.shape[-1]
    halo = recv_buf.shape[2]
    slots = weights_ref.shape[0]
    fb_dev = grad_out.shape[1]
    rows = NOBJ * NVAR
    last = OUTER * INNER - 1
    neighbours = range(len(OFFSETS))
    a = lax.axis_index("dom")
    s = lax.axis_index("sub")

    def shifted(offset):
        return lax.rem(a + offset + n_dom, n_dom)

    pairs = {
        "halo": (halo_hbm, halo_ref), "rhs": (rhs_hbm, rhs_in), "pre": (pre_hbm, pre_ref),
        "cols": (cols_hbm, cols_ref), "jac": (jac_hbm, jac_ref),
        "srd": (srd_hbm, srd_ref), "weights": (weights_hbm, weights_ref),
        "tile": (surf_tile_hbm, surf_tile_ref), "block": (surf_block_hbm, surf_block_ref),
        "count": (count_hbm, count_ref),
    }
    loads = {}
    for number, (name, (src, dst)) in enumerate(pairs.items()):
        loads[name] = pltpu.make_async_copy(src, dst, load_sem.at[number])

    dom_steps = n_dom.bit_length() - 1
    partners = [a + 2 ** k * (1 - 2 * lax.rem(a // 2 ** k, 2)) for k in range(dom_steps)]
    greet = [(shifted(offset), s) for offset in OFFSETS]
    greet += [(partners[k], s) for k in range(2, dom_steps)]
    greet += [(a, lax.rem(s + d, n_sub)) for d in range(1, n_sub)]
    barrier = pltpu.get_barrier_semaphore()
    for device in greet:
        pl.semaphore_signal(barrier, inc=1, device_id=device, device_id_type=MESH)
    for load in loads.values():
        load.start()

    loads["halo"].wait()
    lane = lax.broadcasted_iota(jnp.int32, want_out.shape[1:], 1)
    for k in neighbours:
        demand = jnp.zeros(want_out.shape[1:], jnp.int32)
        for h in range(halo):
            demand = jnp.where(lane == h, halo_ref[h, k], demand)
        want_out[k] = demand
    pl.semaphore_wait(barrier, len(greet))

    def want_copy(k):
        return pltpu.make_async_remote_copy(
            src_ref=want_out.at[k], dst_ref=want_in.at[k],
            send_sem=want_send.at[k], recv_sem=want_recv.at[k],
            device_id=(shifted(-OFFSETS[k]), s), device_id_type=MESH)

    for k in neighbours:
        want_copy(k).start()

    loads["rhs"].wait()
    loads["pre"].wait()

    def first(i, carry):
        residual = []
        for v in range(NVAR):
            value = rhs_in[i, pl.ds(v, NOBJ, stride=NVAR), :]
            rhs_ref[i, v] = value
            residual.append(value)
        for v, change in enumerate(mixed(pre_ref, i, residual)):
            adj_ref[i, v] = change
        return carry

    lax.fori_loop(0, tiles, first, 0)

    def halo_copy(number, k):
        parity = lax.rem(number, 2)
        return pltpu.make_async_remote_copy(
            src_ref=send_buf.at[parity, k], dst_ref=recv_buf.at[parity, k],
            send_sem=halo_send.at[parity, k], recv_sem=halo_recv.at[parity, k],
            device_id=(shifted(OFFSETS[k]), s), device_id_type=MESH)

    def round_own():
        for i in range(tiles):
            ext_ref[i] = adj_ref[i].reshape(rows, cells).astype(jnp.bfloat16)

    for k in neighbours:
        want_copy(k).wait()
    to_smem = pltpu.make_async_copy(want_in, want_ref, want_local)
    to_smem.start()
    to_smem.wait()
    for k in neighbours:
        for h in range(halo):
            tile = adj_ref[want_ref[k, 0, h]]
            send_buf[1, k, h] = tile.reshape(rows, cells).astype(jnp.bfloat16)
        halo_copy(1, k).start()
    round_own()
    for name in ("cols", "jac", "srd", "weights", "tile", "block", "count"):
        loads[name].wait()

    def updated(i):
        picked = jnp.concatenate([ext_ref[cols_ref[b, i]] for b in range(blocks)], axis=1)
        product = jnp.dot(picked, jac_ref[i], preferred_element_type=jnp.float32)
        current = [adj_ref[i, v] for v in range(NVAR)]
        residual = [
            rhs_ref[i, v] - (current[v] + product[v * NOBJ:(v + 1) * NOBJ]) for v in range(NVAR)
        ]
        return [c + change for c, change in zip(current, mixed(pre_ref, i, residual))]

    group = math.gcd(tiles, 4)

    def some(g, carry):
        fresh = [updated(g * group + t) for t in range(group)]
        for t in range(group):
            for v in range(NVAR):
                adj_ref[g * group + t, v] = fresh[t][v]
        return carry

    def receive(number):
        parity = lax.rem(number, 2)
        for k in neighbours:
            halo_copy(number, k).wait()
        for k in neighbours:
            for h in range(halo):
                ext_ref[tiles + k * halo + h] = recv_buf[parity, k, h]

    def design(iteration):
        projected = []
        for u in range(slots):
            alive = jnp.where(u < count_ref[0], 1.0, 0.0).astype(jnp.float32)
            selected = adj_ref[surf_tile_ref[u]]
            parts = []
            for k in range(NDIR):
                total = selected[0] * srd_ref[k, pl.ds(u, 1), :]
                for v in range(1, NVAR):
                    total = total + selected[v] * srd_ref[v * NDIR + k, pl.ds(u, 1), :]
                parts.append(total * alive)
            rounded = jnp.concatenate(parts, axis=0).astype(jnp.bfloat16)
            projected.append(lax.dot_general(
                rounded, weights_ref[u], (((1,), (1,)), ((), ())),
                preferred_element_type=jnp.float32))
        for owner in range(n_sub):
            for f in range(fb_dev):
                total = jnp.zeros_like(projected[0])
                for u in range(slots):
                    chosen = jnp.where(surf_block_ref[u] == owner * fb_dev + f, 1.0, 0.0)
                    total = total + chosen.astype(jnp.float32) * projected[u]
                part_ref[owner, f, iteration] = total

    def sweep(number, carry):
        receive(number)
        for some_neighbours in (neighbours[:2], neighbours[2:]):
            for k in some_neighbours:
                for h in range(halo):
                    fresh = jnp.concatenate(updated(want_ref[k, 0, h]), axis=0)
                    send_buf[lax.rem(number + 1, 2), k, h] = fresh.astype(jnp.bfloat16)
            for k in some_neighbours:
                halo_copy(number + 1, k).start()
        lax.fori_loop(0, tiles // group, some, 0)
        round_own()

        @pl.when(number == INNER - 1)
        def _():
            design(0)

        return carry

    lax.fori_loop(1, last, sweep, 0)
    receive(last)
    lax.fori_loop(0, tiles // group, some, 0)
    design(1)

    def sub_copy(d, f):
        other = lax.rem(s + d, n_sub)
        return pltpu.make_async_remote_copy(
            src_ref=part_ref.at[other, f], dst_ref=sub_buf.at[d - 1, f],
            send_sem=sub_send.at[d - 1, f], recv_sem=sub_recv.at[d - 1, f],
            device_id=(a, other), device_id_type=MESH)

    def dom_copy(k, f):
        return pltpu.make_async_remote_copy(
            src_ref=acc_ref.at[k, f], dst_ref=dom_buf.at[k, f],
            send_sem=dom_send.at[k, f], recv_sem=dom_recv.at[k, f],
            device_id=(partners[(k + f) % dom_steps], s), device_id_type=MESH)

    for f in range(fb_dev):
        for d in range(1, n_sub):
            sub_copy(d, f).start()
    for f in range(fb_dev):
        total = part_ref[s, f]
        for d in range(1, n_sub):
            sub_copy(d, f).wait()
            total = total + sub_buf[d - 1, f]
        acc_ref[0, f] = total
        dom_copy(0, f).start()
    for i in range(tiles):
        for v in range(NVAR):
            adj_out[i, pl.ds(v, NOBJ, stride=NVAR), :] = adj_ref[i, v]
    for k in range(dom_steps):
        for f in range(fb_dev):
            dom_copy(k, f).wait()
            total = acc_ref[k, f] + dom_buf[k, f]
            if k < dom_steps - 1:
                acc_ref[k + 1, f] = total
                dom_copy(k + 1, f).start()
            else:
                total = total * scaling
                for iteration in range(OUTER):
                    for x in range(NDIR):
                        grad_out[iteration, f, pl.ds(x, NOBJ, stride=NDIR), :] = (
                            total[iteration, x * NOBJ:(x + 1) * NOBJ])


def per_device(
    n_dom,
    n_sub,
    block_total,
    jac_blocks,
    block_cols,
    precond,
    right_side,
    halo_rows,
    surface_tile,
    surface_block,
    surface_count,
    surface_residual_derivative,
    lattice_bernstein_weights,
):
    tiles, blocks, cells, _ = jac_blocks.shape
    slots, controls, _ = lattice_bernstein_weights.shape
    neighbours, halo = halo_rows.shape
    fb_dev = block_total // n_sub
    rows = NOBJ * NVAR
    scaling = math.sqrt(fb_dev / (slots * n_dom))
    dom_steps = n_dom.bit_length() - 1
    grad_rows = NOBJ * NDIR
    f32, bf16, i32 = jnp.float32, jnp.bfloat16, jnp.int32
    dma = pltpu.SemaphoreType.DMA
    operands = (
        jac_blocks.reshape(tiles, blocks * cells, cells),
        precond,
        right_side,
        jnp.swapaxes(surface_residual_derivative, 0, 1),
        lattice_bernstein_weights,
        block_cols.T,
        halo_rows.T,
        surface_tile,
        surface_block,
        surface_count,
    )
    vmem = pl.BlockSpec(memory_space=pltpu.VMEM)
    return pl.pallas_call(
        functools.partial(kernel, n_dom, n_sub, scaling),
        out_shape=(
            jax.ShapeDtypeStruct((tiles, rows, cells), f32),
            jax.ShapeDtypeStruct((OUTER, fb_dev, grad_rows, controls), f32),
        ),
        in_specs=[pl.BlockSpec(memory_space=pltpu.HBM)] * len(operands),
        out_specs=(vmem, vmem),
        scratch_shapes=[pltpu.VMEM(x.shape, x.dtype) for x in operands[:5]]
        + [pltpu.SMEM(x.shape, x.dtype) for x in operands[5:]]
        + [
            pltpu.VMEM((tiles, NVAR, NOBJ, cells), f32),
            pltpu.VMEM((tiles, NVAR, NOBJ, cells), f32),
            pltpu.VMEM((tiles + neighbours * halo, rows, cells), bf16),
            pltpu.VMEM((2, neighbours, halo, rows, cells), bf16),
            pltpu.VMEM((2, neighbours, halo, rows, cells), bf16),
            pltpu.VMEM((neighbours, 8, 128), i32),
            pltpu.VMEM((neighbours, 8, 128), i32),
            pltpu.SMEM((neighbours, 8, 128), i32),
            pltpu.VMEM((n_sub, fb_dev, OUTER, grad_rows, controls), f32),
            pltpu.VMEM((n_sub - 1, fb_dev, OUTER, grad_rows, controls), f32),
            pltpu.VMEM((dom_steps, fb_dev, OUTER, grad_rows, controls), f32),
            pltpu.VMEM((dom_steps, fb_dev, OUTER, grad_rows, controls), f32),
            dma((len(operands),)),
            dma((neighbours,)),
            dma((neighbours,)),
            dma,
            dma((2, neighbours)),
            dma((2, neighbours)),
            dma((n_sub - 1, fb_dev)),
            dma((n_sub - 1, fb_dev)),
            dma((dom_steps, fb_dev)),
            dma((dom_steps, fb_dev)),
        ],
        compiler_params=pltpu.CompilerParams(
            collective_id=0, has_side_effects=True, vmem_limit_bytes=60 * 1024 * 1024),
    )(*operands)


FB_DEV = 4


def solution(mesh):
    n_dom, n_sub = mesh.shape["dom"], mesh.shape["sub"]
    both = ("dom", "sub")
    in_specs = (
        P(both, None, None, None),
        P(both, None),
        P(both, None, None),
        P(both, None, None),
        P(both, None),
        P(both),
        P(both),
        P(both),
        P(both, None, None),
        P(both, None, None),
    )
    out_specs = (P(both, None, None), P(None, "sub", None, None))
    return jax.shard_map(
        functools.partial(per_device, n_dom, n_sub, FB_DEV * n_sub),
        mesh=mesh, in_specs=in_specs, out_specs=out_specs, check_vma=False,
    )
```

time: 92.6 us -> 76 us (0.82)
  Pallas kernels: 81.1 us -> 71.4 us
  local copies, waits for them, and re-layouts: 9.79 us -> 3.23 us
    pallas_call x1, Pallas kernels: 81.1 us -> 71.4 us  [per_device(): pl.pallas_call(functools.partial(kernel, n_dom, n_sub, scaling), out_shap...]
    unnamed x17 -> x2, local copies, waits for them, and re-layouts: 9.63 us -> 3.23 us
where the time goes in v2:
time: 76 us; the launch traced here: 75.9 us
  Pallas kernels  71.4 us (94%)
  local copies, waits for them, and re-layouts  3.23 us (4%)
  between operations  1.29 us (2%)
    pallas_call x1, Pallas kernels, per_device(): pl.pallas_call(functools.partial(kernel, n_dom, n_sub, scaling), out_shap...  71.4 us
    unnamed x2, local copies, waits for them, and re-layouts  3.23 us

profile of v2, /device:TPU:0, one launch (start us, length us, event | category | flops | bytes accessed | tf_op | source)
XLA Modules:
  0.0 75.9 jit_solution(13368473762740639002)
XLA Ops:
  1.3 71.4 %shard_map.113 = (f32[12,48,128]{2,1,0:T(8,128)}, f32[2,4,24,128]{3,2,1,0:T(8,128)}) custom-call(bf16[12,768,128]{2,1,0:T(8,128)(2,1)} %bitcast.4, f32[12,36,128]{2,1,0:T(8,128)} %pre_hbm.1, f32[12,48,128]{2,1,0:T(8,128)} %rhs_hbm.1, f32[18,8,128]{2,1,0:T(8,128)} %bitcast.5, bf16[8,128,128]{2,1,0:T(8,128)(2,1)} %weights_hbm.1, s32[6,12]{1,0:T(8,128)} %bitcast.6, ...), custom_call_target="tpu_custom_call" | custom-call | tf_op jit(solution)/shard_map/pallas_call | solution.py:290
  72.7 1.7 %copy.15 = f32[12,48,128]{2,1,0:T(8,128)} copy(f32[12,48,128]{2,1,0:T(8,128)} %get-tuple-element.4) | data formatting | bytes 589824
  74.4 1.5 %copy.16 = f32[2,4,24,128]{3,2,1,0:T(8,128)} copy(f32[2,4,24,128]{3,2,1,0:T(8,128)} %get-tuple-element.5) | data formatting | bytes 196608

commit v3 on v2

--- a/solution.py
+++ b/solution.py
@@ -24,7 +24,7 @@
     for v in range(NVAR):
         total = RELAXATION * residual[v]
         for w in range(NVAR):
-            total = total + pre_ref[tile, pl.ds(v * NVAR + w, 1), :] * residual[w]
+            total = total + pre_ref[tile, v * NVAR + w] * residual[w]
         out.append(total)
     return out
 
@@ -34,9 +34,9 @@
     jac_hbm, pre_hbm, rhs_hbm, srd_hbm, weights_hbm,
     cols_hbm, halo_hbm, surf_tile_hbm, surf_block_hbm, count_hbm,
     adj_out, grad_out,
-    jac_ref, pre_ref, rhs_in, srd_ref, weights_ref,
+    jac_ref, pre_in, rhs_in, srd_ref, weights_ref,
     cols_ref, halo_ref, surf_tile_ref, surf_block_ref, count_ref,
-    rhs_ref, adj_ref, ext_ref, send_buf, recv_buf,
+    pre_ref, rhs_ref, adj_ref, ext_ref, send_buf, recv_buf,
     want_out, want_in, want_ref,
     part_ref, sub_buf, acc_ref, dom_buf,
     load_sem, want_send, want_recv, want_local, halo_send, halo_recv,
@@ -57,7 +57,7 @@
         return lax.rem(a + offset + n_dom, n_dom)
 
     pairs = {
-        "halo": (halo_hbm, halo_ref), "rhs": (rhs_hbm, rhs_in), "pre": (pre_hbm, pre_ref),
+        "halo": (halo_hbm, halo_ref), "rhs": (rhs_hbm, rhs_in), "pre": (pre_hbm, pre_in),
         "cols": (cols_hbm, cols_ref), "jac": (jac_hbm, jac_ref),
         "srd": (srd_hbm, srd_ref), "weights": (weights_hbm, weights_ref),
         "tile": (surf_tile_hbm, surf_tile_ref), "block": (surf_block_hbm, surf_block_ref),
@@ -100,6 +100,9 @@
     loads["pre"].wait()
 
     def first(i, carry):
+        for row in range(NVAR * NVAR):
+            spread = jnp.broadcast_to(pre_in[i, pl.ds(row, 1), :], (NOBJ, cells))
+            pre_ref[i, row] = spread
         residual = []
         for v in range(NVAR):
             value = rhs_in[i, pl.ds(v, NOBJ, stride=NVAR), :]
@@ -145,14 +148,10 @@
         ]
         return [c + change for c, change in zip(current, mixed(pre_ref, i, residual))]
 
-    group = math.gcd(tiles, 4)
-
-    def some(g, carry):
-        fresh = [updated(g * group + t) for t in range(group)]
-        for t in range(group):
-            for v in range(NVAR):
-                adj_ref[g * group + t, v] = fresh[t][v]
-        return carry
+    def update_own():
+        for i in range(tiles):
+            for v, value in enumerate(updated(i)):
+                adj_ref[i, v] = value
 
     def receive(number):
         parity = lax.rem(number, 2)
@@ -194,7 +193,7 @@
                     send_buf[lax.rem(number + 1, 2), k, h] = fresh.astype(jnp.bfloat16)
             for k in some_neighbours:
                 halo_copy(number + 1, k).start()
-        lax.fori_loop(0, tiles // group, some, 0)
+        update_own()
         round_own()
 
         @pl.when(number == INNER - 1)
@@ -205,7 +204,7 @@
 
     lax.fori_loop(1, last, sweep, 0)
     receive(last)
-    lax.fori_loop(0, tiles // group, some, 0)
+    update_own()
     design(1)
 
     def sub_copy(d, f):
@@ -298,6 +297,7 @@
         scratch_shapes=[pltpu.VMEM(x.shape, x.dtype) for x in operands[:5]]
         + [pltpu.SMEM(x.shape, x.dtype) for x in operands[5:]]
         + [
+            pltpu.VMEM((tiles, NVAR * NVAR, NOBJ, cells), f32),
             pltpu.VMEM((tiles, NVAR, NOBJ, cells), f32),
             pltpu.VMEM((tiles, NVAR, NOBJ, cells), f32),
             pltpu.VMEM((tiles + neighbours * halo, rows, cells), bf16),

time: 76 us -> 75.8 us (level)
  no operation moved by 1% of the time
where the time goes in v3:
time: 75.8 us; the launch traced here: 75.6 us
  Pallas kernels  71.1 us (94%)
  local copies, waits for them, and re-layouts  3.23 us (4%)
  between operations  1.29 us (2%)
    pallas_call x1, Pallas kernels, per_device(): pl.pallas_call(functools.partial(kernel, n_dom, n_sub, scaling), out_shap...  71.1 us
    unnamed x2, local copies, waits for them, and re-layouts  3.23 us

profile of v3, /device:TPU:0, one launch (start us, length us, event | category | flops | bytes accessed | tf_op | source)
XLA Modules:
  0.0 75.6 jit_solution(6387260712805452334)
XLA Ops:
  1.3 71.1 %shard_map.113 = (f32[12,48,128]{2,1,0:T(8,128)}, f32[2,4,24,128]{3,2,1,0:T(8,128)}) custom-call(bf16[12,768,128]{2,1,0:T(8,128)(2,1)} %bitcast.4, f32[12,36,128]{2,1,0:T(8,128)} %pre_hbm.1, f32[12,48,128]{2,1,0:T(8,128)} %rhs_hbm.1, f32[18,8,128]{2,1,0:T(8,128)} %bitcast.5, bf16[8,128,128]{2,1,0:T(8,128)(2,1)} %weights_hbm.1, s32[6,12]{1,0:T(8,128)} %bitcast.6, ...), custom_call_target="tpu_custom_call" | custom-call | tf_op jit(solution)/shard_map/pallas_call | solution.py:289
  72.4 1.7 %copy.15 = f32[12,48,128]{2,1,0:T(8,128)} copy(f32[12,48,128]{2,1,0:T(8,128)} %get-tuple-element.4) | data formatting | bytes 589824
  74.1 1.5 %copy.16 = f32[2,4,24,128]{3,2,1,0:T(8,128)} copy(f32[2,4,24,128]{3,2,1,0:T(8,128)} %get-tuple-element.5) | data formatting | bytes 196608

commit v4 on v3

--- a/solution.py
+++ b/solution.py
@@ -182,10 +182,54 @@
                 for u in range(slots):
                     chosen = jnp.where(surf_block_ref[u] == owner * fb_dev + f, 1.0, 0.0)
                     total = total + chosen.astype(jnp.float32) * projected[u]
-                part_ref[owner, f, iteration] = total
+                part_ref[iteration, owner, f] = total
+
+    def sub_copy(iteration, d, f):
+        other = lax.rem(s + d, n_sub)
+        return pltpu.make_async_remote_copy(
+            src_ref=part_ref.at[iteration, other, f], dst_ref=sub_buf.at[iteration, d - 1, f],
+            send_sem=sub_send.at[iteration, d - 1, f], recv_sem=sub_recv.at[iteration, d - 1, f],
+            device_id=(a, other), device_id_type=MESH)
+
+    def dom_copy(iteration, k, f):
+        return pltpu.make_async_remote_copy(
+            src_ref=acc_ref.at[iteration, k, f], dst_ref=dom_buf.at[iteration, k, f],
+            send_sem=dom_send.at[iteration, k, f], recv_sem=dom_recv.at[iteration, k, f],
+            device_id=(partners[(k + f) % dom_steps], s), device_id_type=MESH)
+
+    def send_partials(iteration):
+        for f in range(fb_dev):
+            for d in range(1, n_sub):
+                sub_copy(iteration, d, f).start()
+
+    def finish_stage(iteration, stage):
+        for f in range(fb_dev):
+            if stage == 0:
+                total = part_ref[iteration, s, f]
+                for d in range(1, n_sub):
+                    sub_copy(iteration, d, f).wait()
+                    total = total + sub_buf[iteration, d - 1, f]
+            else:
+                dom_copy(iteration, stage - 1, f).wait()
+                total = acc_ref[iteration, stage - 1, f] + dom_buf[iteration, stage - 1, f]
+            if stage < dom_steps:
+                acc_ref[iteration, stage, f] = total
+                dom_copy(iteration, stage, f).start()
+            else:
+                total = total * scaling
+                for x in range(NDIR):
+                    grad_out[iteration, f, pl.ds(x, NOBJ, stride=NDIR), :] = (
+                        total[x * NOBJ:(x + 1) * NOBJ])
+
+    beside = min(dom_steps + 1, last - INNER)
 
     def sweep(number, carry):
         receive(number)
+        for stage in range(beside):
+            @pl.when(number == INNER + stage)
+            def _():
+                finish_stage(0, stage)
+
         for some_neighbours in (neighbours[:2], neighbours[2:]):
             for k in some_neighbours:
                 for h in range(halo):
@@ -199,6 +243,7 @@
         @pl.when(number == INNER - 1)
         def _():
             design(0)
+            send_partials(0)
 
         return carry
 
@@ -206,46 +251,14 @@
     receive(last)
     update_own()
     design(1)
-
-    def sub_copy(d, f):
-        other = lax.rem(s + d, n_sub)
-        return pltpu.make_async_remote_copy(
-            src_ref=part_ref.at[other, f], dst_ref=sub_buf.at[d - 1, f],
-            send_sem=sub_send.at[d - 1, f], recv_sem=sub_recv.at[d - 1, f],
-            device_id=(a, other), device_id_type=MESH)
-
-    def dom_copy(k, f):
-        return pltpu.make_async_remote_copy(
-            src_ref=acc_ref.at[k, f], dst_ref=dom_buf.at[k, f],
-            send_sem=dom_send.at[k, f], recv_sem=dom_recv.at[k, f],
-            device_id=(partners[(k + f) % dom_steps], s), device_id_type=MESH)
-
-    for f in range(fb_dev):
-        for d in range(1, n_sub):
-            sub_copy(d, f).start()
-    for f in range(fb_dev):
-        total = part_ref[s, f]
-        for d in range(1, n_sub):
-            sub_copy(d, f).wait()
-            total = total + sub_buf[d - 1, f]
-        acc_ref[0, f] = total
-        dom_copy(0, f).start()
+    send_partials(1)
     for i in range(tiles):
         for v in range(NVAR):
             adj_out[i, pl.ds(v, NOBJ, stride=NVAR), :] = adj_ref[i, v]
-    for k in range(dom_steps):
-        for f in range(fb_dev):
-            dom_copy(k, f).wait()
-            total = acc_ref[k, f] + dom_buf[k, f]
-            if k < dom_steps - 1:
-                acc_ref[k + 1, f] = total
-                dom_copy(k + 1, f).start()
-            else:
-                total = total * scaling
-                for iteration in range(OUTER):
-                    for x in range(NDIR):
-                        grad_out[iteration, f, pl.ds(x, NOBJ, stride=NDIR), :] = (
-                            total[iteration, x * NOBJ:(x + 1) * NOBJ])
+    for stage in range(beside, dom_steps + 1):
+        finish_stage(0, stage)
+    for stage in range(dom_steps + 1):
+        finish_stage(1, stage)
 
 
 def per_device(
@@ -306,20 +319,20 @@
             pltpu.VMEM((neighbours, 8, 128), i32),
             pltpu.VMEM((neighbours, 8, 128), i32),
             pltpu.SMEM((neighbours, 8, 128), i32),
-            pltpu.VMEM((n_sub, fb_dev, OUTER, grad_rows, controls), f32),
-            pltpu.VMEM((n_sub - 1, fb_dev, OUTER, grad_rows, controls), f32),
-            pltpu.VMEM((dom_steps, fb_dev, OUTER, grad_rows, controls), f32),
-            pltpu.VMEM((dom_steps, fb_dev, OUTER, grad_rows, controls), f32),
+            pltpu.VMEM((OUTER, n_sub, fb_dev, grad_rows, controls), f32),
+            pltpu.VMEM((OUTER, n_sub - 1, fb_dev, grad_rows, controls), f32),
+            pltpu.VMEM((OUTER, dom_steps, fb_dev, grad_rows, controls), f32),
+            pltpu.VMEM((OUTER, dom_steps, fb_dev, grad_rows, controls), f32),
             dma((len(operands),)),
             dma((neighbours,)),
             dma((neighbours,)),
             dma,
             dma((2, neighbours)),
             dma((2, neighbours)),
-            dma((n_sub - 1, fb_dev)),
-            dma((n_sub - 1, fb_dev)),
-            dma((dom_steps, fb_dev)),
-            dma((dom_steps, fb_dev)),
+            dma((OUTER, n_sub - 1, fb_dev)),
+            dma((OUTER, n_sub - 1, fb_dev)),
+            dma((OUTER, dom_steps, fb_dev)),
+            dma((OUTER, dom_steps, fb_dev)),
         ],
         compiler_params=pltpu.CompilerParams(
             collective_id=0, has_side_effects=True, vmem_limit_bytes=60 * 1024 * 1024),

time: 75.8 us -> 76.6 us (1.011)
  Pallas kernels: 71.1 us -> 71.9 us
    pallas_call x1, Pallas kernels: 71.1 us -> 71.9 us  [per_device(): pl.pallas_call(functools.partial(kernel, n_dom, n_sub, scaling), out_shap...]
where the time goes in v4:
time: 76.6 us; the launch traced here: 76.4 us
  Pallas kernels  71.9 us (94%)
  local copies, waits for them, and re-layouts  3.23 us (4%)
  between operations  1.29 us (2%)
    pallas_call x1, Pallas kernels, per_device(): pl.pallas_call(functools.partial(kernel, n_dom, n_sub, scaling), out_shap...  71.9 us
    unnamed x2, local copies, waits for them, and re-layouts  3.23 us

profile of v4, /device:TPU:0, one launch (start us, length us, event | category | flops | bytes accessed | tf_op | source)
XLA Modules:
  0.0 76.4 jit_solution(3567480976061668199)
XLA Ops:
  1.3 71.9 %shard_map.113 = (f32[12,48,128]{2,1,0:T(8,128)}, f32[2,4,24,128]{3,2,1,0:T(8,128)}) custom-call(bf16[12,768,128]{2,1,0:T(8,128)(2,1)} %bitcast.4, f32[12,36,128]{2,1,0:T(8,128)} %pre_hbm.1, f32[12,48,128]{2,1,0:T(8,128)} %rhs_hbm.1, f32[18,8,128]{2,1,0:T(8,128)} %bitcast.5, bf16[8,128,128]{2,1,0:T(8,128)(2,1)} %weights_hbm.1, s32[6,12]{1,0:T(8,128)} %bitcast.6, ...), custom_call_target="tpu_custom_call" | custom-call | tf_op jit(solution)/shard_map/pallas_call | solution.py:302
  73.1 1.7 %copy.15 = f32[12,48,128]{2,1,0:T(8,128)} copy(f32[12,48,128]{2,1,0:T(8,128)} %get-tuple-element.4) | data formatting | bytes 589824
  74.8 1.5 %copy.16 = f32[2,4,24,128]{3,2,1,0:T(8,128)} copy(f32[2,4,24,128]{3,2,1,0:T(8,128)} %get-tuple-element.5) | data formatting | bytes 196608
